TPU v7x, 32 devices: a whole 2x2x4 slice. The times are simulated.
32 devices in a mesh: dp: 8 (over y, x, core), tensor: 4 (over z).
Axes of the slice: x: 2, y: 2, z: 4, core: 2. Of those that a mesh axis runs over, the one named last changes fastest.
Arguments:
- inputs: float32 [16384, 1024], P(('dp', 'tensor')), may hold values from -6 to 6
- lengths: int32 [8, 4], P('dp'), may hold values from 0 to 2048, as said below
- ln_gain: float32 [2, 2, 1024], replicated, may hold values from 0.1 to 1.9
- ln_bias: float32 [2, 2, 1024], replicated, may hold values from -4 to 4
- out_bias: float32 [2, 2, 1024], replicated, may hold values from -6 to 6
- w_qkv: bfloat16 [2, 1024, 3, 1024], P(None, None, None, 'tensor'), may hold values from -0.1875 to 0.1875
- qv_bias: float32 [2, 2, 1024], P(None, None, 'tensor'), may hold values from -6 to 6
- w_out: bfloat16 [2, 1024, 1024], P(None, 'tensor'), may hold values from -2 to 2
- w_in: bfloat16 [2, 1024, 4096], P(None, None, 'tensor'), may hold values from -0.1875 to 0.1875
- in_bias: float32 [2, 4096], P(None, 'tensor'), may hold values from -6 to 6
- w_down: bfloat16 [2, 4096, 1024], P(None, 'tensor'), may hold values from -0.09375 to 0.09375
- out_grad: float32 [16384, 1024], P(('dp', 'tensor')), may hold values from -6 to 6
Outputs:
- outputs: float32 [16384, 1024], P(('dp', 'tensor'))
- input_grad: float32 [16384, 1024], P(('dp', 'tensor'))
- grad_ln_gain: float32 [2, 2, 1024], P(None, None, ('dp', 'tensor'))
- grad_ln_bias: float32 [2, 2, 1024], P(None, None, ('dp', 'tensor'))
- grad_out_bias: float32 [2, 2, 1024], P(None, None, ('dp', 'tensor'))
- grad_w_qkv: float32 [2, 1024, 3, 1024], P(None, 'dp', None, 'tensor')
- grad_qv_bias: float32 [2, 2, 1024], P(None, None, ('tensor', 'dp'))
- grad_w_out: float32 [2, 1024, 1024], P(None, 'tensor', 'dp')
- grad_w_in: float32 [2, 1024, 4096], P(None, 'dp', 'tensor')
- grad_in_bias: float32 [2, 4096], P(None, ('tensor', 'dp'))
- grad_w_down: float32 [2, 4096, 1024], P(None, 'tensor', 'dp')
Inputs may be any that keep to these rules, and one draw needn't show every extreme that they name: In each group the 4 lengths sum to 2048, and the group's documents lie in its rows in the order of its lengths; some lengths are zero.
All inputs are finite; a program needn't handle non-finite values.
Results may differ from a plain program's by a relative error of at most 0.02.
Values may be sent and summed in bfloat16 or wider, within the bound.
A program may use at most 320 MiB of HBM per device.

v0:
```python
import jax
import jax.numpy as jnp
from jax import lax
from jax.sharding import PartitionSpec as P

D = 1024
HEAD = 128
LAYERS = 2


EPS = 1e-05
NEG = -1e30


def layer_norm(values, gain_vec, bias_vec):
    centre = values - jnp.mean(values, -1, keepdims=True)
    spread = jnp.mean(centre * centre, -1, keepdims=True)
    return centre * lax.rsqrt(spread + EPS) * gain_vec + bias_vec


def contract_rows(left, right):
    return lax.dot_general(
        left, right, (((0,), (0,)), ((), ())), preferred_element_type=jnp.float32
    )


def contract_cols(left, right):
    return lax.dot_general(
        left, right, (((1,), (1,)), ((), ())), preferred_element_type=jnp.float32
    )


def segment_ids(lengths_row, tokens):
    doc_ends = jnp.cumsum(lengths_row)
    positions = jnp.arange(tokens, dtype=jnp.int32)
    return jnp.sum((positions[:, None] >= doc_ends[None, :]).astype(jnp.int32), 1)


def block_mask(seg_ids, row_start, row_stop):
    positions = jnp.arange(row_stop, dtype=jnp.int32)
    row_ids = positions[row_start:row_stop]
    same_doc = seg_ids[row_start:row_stop, None] == seg_ids[None, :row_stop]
    return same_doc & (positions[None, :] <= row_ids[:, None])


def attend_forward(queries, key_rows, value_rows, seg_ids):
    tokens = queries.shape[0]
    block_len = min(512, tokens)
    score_scale = float(HEAD) ** (-0.5)
    outputs_list = []
    sums_list = []
    for block_id in range(tokens // block_len):
        row_start = block_id * block_len
        row_stop = row_start + block_len
        scores = (
            jnp.einsum(
                "qhd,khd->hqk",
                queries[row_start:row_stop],
                key_rows[:row_stop],
                preferred_element_type=jnp.float32,
            )
            * score_scale
        )
        scores = jnp.where(block_mask(seg_ids, row_start, row_stop)[None], scores, NEG)
        largest = jnp.max(scores, -1, keepdims=True)
        expo = jnp.exp(scores - largest)
        totals = jnp.sum(expo, -1, keepdims=True)
        weights = (expo / totals).astype(jnp.bfloat16)
        outputs_list.append(
            jnp.einsum(
                "hqk,khd->qhd", weights, value_rows[:row_stop], preferred_element_type=jnp.float32
            )
        )
        sums_list.append((largest + jnp.log(totals))[..., 0])
    return (jnp.concatenate(outputs_list, 0), jnp.concatenate(sums_list, 1))


def attend_backward(queries, key_rows, value_rows, seg_ids, log_sums, grad_out):
    tokens = queries.shape[0]
    block_len = min(512, tokens)
    score_scale = float(HEAD) ** (-0.5)
    grad_keys = jnp.zeros(key_rows.shape, jnp.float32)
    grad_values = jnp.zeros(value_rows.shape, jnp.float32)
    grad_queries = []
    for block_id in range(tokens // block_len):
        row_start = block_id * block_len
        row_stop = row_start + block_len
        q_rows = queries[row_start:row_stop]
        out_rows = grad_out[row_start:row_stop]
        scores = (
            jnp.einsum(
                "qhd,khd->hqk", q_rows, key_rows[:row_stop], preferred_element_type=jnp.float32
            )
            * score_scale
        )
        scores = jnp.where(block_mask(seg_ids, row_start, row_stop)[None], scores, NEG)
        probs = jnp.exp(scores - log_sums[:, row_start:row_stop, None])
        grad_probs = jnp.einsum(
            "qhd,khd->hqk", out_rows, value_rows[:row_stop], preferred_element_type=jnp.float32
        )
        inner_sum = jnp.sum(probs * grad_probs, -1, keepdims=True)
        grad_scores = (probs * (grad_probs - inner_sum) * score_scale).astype(jnp.bfloat16)
        grad_queries.append(
            jnp.einsum(
                "hqk,khd->qhd", grad_scores, key_rows[:row_stop], preferred_element_type=jnp.float32
            )
        )
        grad_keys = grad_keys.at[:row_stop].add(
            jnp.einsum("hqk,qhd->khd", grad_scores, q_rows, preferred_element_type=jnp.float32)
        )
        grad_values = grad_values.at[:row_stop].add(
            jnp.einsum(
                "hqk,qhd->khd",
                probs.astype(jnp.bfloat16),
                out_rows,
                preferred_element_type=jnp.float32,
            )
        )
    return (jnp.concatenate(grad_queries, 0), grad_keys, grad_values)


def gather_normed(normed):
    return lax.all_gather(normed, "tensor", axis=0, tiled=True)


def feed_sum(active, weight):
    return lax.psum_scatter(
        jnp.dot(active, weight, preferred_element_type=jnp.float32).astype(jnp.bfloat16),
        "tensor",
        scatter_dimension=0,
        tiled=True,
    ).astype(jnp.float32)


def input_sum(grads, weight):
    return lax.psum_scatter(
        contract_cols(grads, weight).astype(jnp.bfloat16), "tensor", scatter_dimension=0, tiled=True
    ).astype(jnp.float32)


def on_device(
    inputs,
    lengths,
    ln_gain,
    ln_bias,
    out_bias,
    w_qkv,
    qv_bias,
    w_out,
    w_in,
    in_bias,
    w_down,
    out_grad,
):
    dev_rows = inputs.shape[0]
    tokens = dev_rows * lax.axis_size("tensor")
    inner = qv_bias.shape[2]
    local_heads = inner // HEAD
    head_shape = (tokens, local_heads, HEAD)
    seg_ids = segment_ids(lengths[0], tokens)
    stream = inputs
    kept = []
    for layer_id in range(LAYERS):
        normed = layer_norm(stream, ln_gain[layer_id, 0], ln_bias[layer_id, 0]).astype(jnp.bfloat16)
        full_one = gather_normed(normed)
        projected = jnp.dot(
            full_one, w_qkv[layer_id].reshape(D, 3 * inner), preferred_element_type=jnp.float32
        )
        queries = (
            (projected[:, :inner] + qv_bias[layer_id, 0]).astype(jnp.bfloat16).reshape(head_shape)
        )
        key_rows = projected[:, inner : 2 * inner].astype(jnp.bfloat16).reshape(head_shape)
        value_rows = (
            (projected[:, 2 * inner :] + qv_bias[layer_id, 1])
            .astype(jnp.bfloat16)
            .reshape(head_shape)
        )
        attended, log_sums = attend_forward(queries, key_rows, value_rows, seg_ids)
        attended = attended.reshape(tokens, inner).astype(jnp.bfloat16)
        out_full = lax.all_gather(w_out[layer_id], "tensor", axis=0, tiled=True)
        head_rows = lax.all_to_all(attended, "tensor", split_axis=0, concat_axis=1, tiled=True)
        branch = jnp.dot(head_rows, out_full, preferred_element_type=jnp.float32)
        middle = stream + branch + out_bias[layer_id, 0]
        normed_two = layer_norm(middle, ln_gain[layer_id, 1], ln_bias[layer_id, 1]).astype(
            jnp.bfloat16
        )
        full_two = gather_normed(normed_two)
        hidden = (
            jnp.dot(full_two, w_in[layer_id], preferred_element_type=jnp.float32)
            + in_bias[layer_id]
        )
        active = jax.nn.gelu(hidden).astype(jnp.bfloat16)
        kept.append(
            (
                stream,
                full_one,
                queries,
                key_rows,
                value_rows,
                log_sums,
                head_rows,
                out_full,
                middle,
                full_two,
                hidden,
                active,
            )
        )
        stream = middle + feed_sum(active, w_down[layer_id]) + out_bias[layer_id, 1]
    grad = out_grad
    per_layer = [None] * LAYERS
    for layer_id in reversed(range(LAYERS)):
        (
            entry,
            full_one,
            queries,
            key_rows,
            value_rows,
            log_sums,
            head_rows,
            out_full,
            middle,
            full_two,
            hidden,
            active,
        ) = kept[layer_id]
        bias_two = jnp.sum(grad, 0)
        grad_low = grad.astype(jnp.bfloat16)
        grad_full = lax.all_gather(grad_low, "tensor", axis=0, tiled=True)
        grad_down = contract_rows(active, grad_full)
        grad_active = contract_cols(grad_full, w_down[layer_id])
        gelu_value, gelu_pull = jax.vjp(jax.nn.gelu, hidden)
        grad_hidden = gelu_pull(grad_active)[0].astype(jnp.bfloat16)
        bias_in = jnp.sum(grad_hidden, 0, dtype=jnp.float32)
        grad_up = contract_rows(full_two, grad_hidden)
        grad_normed = input_sum(grad_hidden, w_in[layer_id])
        norm_value, norm_pull = jax.vjp(
            layer_norm, middle, ln_gain[layer_id, 1], ln_bias[layer_id, 1]
        )
        grad_middle, gain_two, shift_two = norm_pull(grad_normed)
        grad = grad + grad_middle
        bias_one = jnp.sum(grad, 0)
        grad_mid_low = grad.astype(jnp.bfloat16)
        grad_proj_w = lax.psum_scatter(
            contract_rows(head_rows, grad_mid_low).astype(jnp.bfloat16),
            "tensor",
            scatter_dimension=0,
            tiled=True,
        ).astype(jnp.float32)
        grad_heads = contract_cols(grad_mid_low, out_full).astype(jnp.bfloat16)
        grad_attended = lax.all_to_all(
            grad_heads, "tensor", split_axis=1, concat_axis=0, tiled=True
        )
        grad_q, grad_k, grad_v = attend_backward(
            queries, key_rows, value_rows, seg_ids, log_sums, grad_attended.reshape(head_shape)
        )
        low_q = grad_q.astype(jnp.bfloat16).reshape(tokens, inner)
        low_k = grad_k.astype(jnp.bfloat16).reshape(tokens, inner)
        low_v = grad_v.astype(jnp.bfloat16).reshape(tokens, inner)
        grad_mixed = jnp.concatenate([low_q, low_k, low_v], 1)
        grad_qkv_w = contract_rows(full_one, grad_mixed).reshape(D, 3, inner)
        grad_qv = jnp.stack(
            [jnp.sum(low_q, 0, dtype=jnp.float32), jnp.sum(low_v, 0, dtype=jnp.float32)]
        )
        grad_normed_one = input_sum(grad_mixed, w_qkv[layer_id].reshape(D, 3 * inner))
        norm_value, norm_pull = jax.vjp(
            layer_norm, entry, ln_gain[layer_id, 0], ln_bias[layer_id, 0]
        )
        grad_entry, gain_one, shift_one = norm_pull(grad_normed_one)
        grad = grad + grad_entry
        per_layer[layer_id] = (
            jnp.stack([gain_one, gain_two]),
            jnp.stack([shift_one, shift_two]),
            jnp.stack([bias_one, bias_two]),
            grad_qkv_w,
            grad_qv,
            grad_proj_w,
            grad_up,
            bias_in,
            grad_down,
        )
    gain_all = jnp.stack([entry_grads[0] for entry_grads in per_layer])
    shift_all = jnp.stack([entry_grads[1] for entry_grads in per_layer])
    outb_all = jnp.stack([entry_grads[2] for entry_grads in per_layer])
    qkv_all = jnp.stack([entry_grads[3] for entry_grads in per_layer])
    qvb_all = jnp.stack([entry_grads[4] for entry_grads in per_layer])
    proj_all = jnp.stack([entry_grads[5] for entry_grads in per_layer])
    up_all = jnp.stack([entry_grads[6] for entry_grads in per_layer])
    inb_all = jnp.stack([entry_grads[7] for entry_grads in per_layer])
    down_all = jnp.stack([entry_grads[8] for entry_grads in per_layer])
    qkv_sum, qvb_sum, proj_sum, up_sum, inb_sum, down_sum = (
        lax.psum_scatter(
            qkv_all.astype(jnp.bfloat16), "dp", scatter_dimension=1, tiled=True
        ).astype(jnp.float32),
        lax.psum_scatter(
            qvb_all.astype(jnp.bfloat16), "dp", scatter_dimension=2, tiled=True
        ).astype(jnp.float32),
        lax.psum_scatter(
            proj_all.astype(jnp.bfloat16), "dp", scatter_dimension=2, tiled=True
        ).astype(jnp.float32),
        lax.psum_scatter(up_all.astype(jnp.bfloat16), "dp", scatter_dimension=1, tiled=True).astype(
            jnp.float32
        ),
        lax.psum_scatter(
            inb_all.astype(jnp.bfloat16), "dp", scatter_dimension=1, tiled=True
        ).astype(jnp.float32),
        lax.psum_scatter(
            down_all.astype(jnp.bfloat16), "dp", scatter_dimension=2, tiled=True
        ).astype(jnp.float32),
    )
    gain_sum, shift_sum, outb_sum = (
        lax.psum_scatter(gain_all, ("dp", "tensor"), scatter_dimension=2, tiled=True),
        lax.psum_scatter(shift_all, ("dp", "tensor"), scatter_dimension=2, tiled=True),
        lax.psum_scatter(outb_all, ("dp", "tensor"), scatter_dimension=2, tiled=True),
    )
    return (
        stream,
        grad,
        gain_sum,
        shift_sum,
        outb_sum,
        qkv_sum,
        qvb_sum,
        proj_sum,
        up_sum,
        inb_sum,
        down_sum,
    )


def solution(mesh):
    return jax.shard_map(
        on_device,
        mesh=mesh,
        in_specs=(
            P(("dp", "tensor"), None),
            P("dp", None),
            P(),
            P(),
            P(),
            P(None, None, None, "tensor"),
            P(None, None, "tensor"),
            P(None, "tensor", None),
            P(None, None, "tensor"),
            P(None, "tensor"),
            P(None, "tensor", None),
            P(("dp", "tensor"), None),
        ),
        out_specs=(
            P(("dp", "tensor"), None),
            P(("dp", "tensor"), None),
            P(None, None, ("dp", "tensor")),
            P(None, None, ("dp", "tensor")),
            P(None, None, ("dp", "tensor")),
            P(None, "dp", None, "tensor"),
            P(None, None, ("tensor", "dp")),
            P(None, "tensor", "dp"),
            P(None, "dp", "tensor"),
            P(None, ("tensor", "dp")),
            P(None, "tensor", "dp"),
        ),
        check_vma=False,
    )
```

profile of v0, /device:TPU:0, one launch (start us, length us, event | category | flops | bytes accessed | tf_op | source)
XLA Modules:
  0.0 2165.3 jit_solution(13897676013780759789)
XLA Ops:
  22.7 74.2 %all-gather.11.cloned.1.call-done = bf16[2048,1024]{1,0:T(8,128)(2,1)} async-done(((bf16[512,1024]{1,0:T(8,128)(2,1)}), bf16[2048,1024]{1,0:T(8,128)(2,1)}) %all-gather.11.cloned.1.call-update) | async-done | bytes 4194320 | tf_op jit(solution)/shard_map/all_gather | solution.py:123
  126.5 34.9 %all-gather.23.cloned.1.call-done = bf16[1,1024,1024]{2,1,0:T(8,128)(2,1)} async-done(((bf16[1,256,1024]{2,1,0:T(8,128)(2,1)}), bf16[1,1024,1024]{2,1,0:T(8,128)(2,1)}) %all-gather.23.cloned.1.call-update) | async-done | bytes 2097168 | tf_op jit(solution)/shard_map/all_gather | solution.py:180
  171.4 79.5 %all-gather.13.cloned.1.call-done = bf16[2048,1024]{1,0:T(8,128)(2,1)} async-done(((bf16[512,1024]{1,0:T(8,128)(2,1)}), bf16[2048,1024]{1,0:T(8,128)(2,1)}) %all-gather.13.cloned.1.call-update) | async-done | bytes 4194320 | tf_op jit(solution)/shard_map/all_gather | solution.py:123
  268.4 75.2 %reduce-scatter.32.cloned.1.call-done = bf16[512,1024]{1,0:T(8,128)(2,1)} async-done(((bf16[2048,1024]{1,0:T(8,128)(2,1)}), bf16[512,1024]{1,0:T(8,128)(2,1)}) %reduce-scatter.32.cloned.1.call-update) | async-done | bytes 1048592 | tf_op jit(solution)/shard_map/reduce_scatter | solution.py:127
  349.4 80.0 %all-gather.15.cloned.1.call-done = bf16[2048,1024]{1,0:T(8,128)(2,1)} async-done(((bf16[512,1024]{1,0:T(8,128)(2,1)}), bf16[2048,1024]{1,0:T(8,128)(2,1)}) %all-gather.15.cloned.1.call-update) | async-done | bytes 4194320 | tf_op jit(solution)/shard_map/all_gather | solution.py:123
  463.3 21.9 %all-gather.25.cloned.1.call-done = bf16[1,1024,1024]{2,1,0:T(8,128)(2,1)} async-done(((bf16[1,256,1024]{2,1,0:T(8,128)(2,1)}), bf16[1,1024,1024]{2,1,0:T(8,128)(2,1)}) %all-gather.25.cloned.1.call-update) | async-done | bytes 2097168 | tf_op jit(solution)/shard_map/all_gather | solution.py:180
  507.9 75.3 %all-gather.17.cloned.1.call-done = bf16[2048,1024]{1,0:T(8,128)(2,1)} async-done(((bf16[512,1024]{1,0:T(8,128)(2,1)}), bf16[2048,1024]{1,0:T(8,128)(2,1)}) %all-gather.17.cloned.1.call-update) | async-done | bytes 4194320 | tf_op jit(solution)/shard_map/all_gather | solution.py:123
  594.1 70.6 %all-gather.19.cloned.1.call-done = bf16[2048,1024]{1,0:T(8,128)(2,1)} async-done(((bf16[512,1024]{1,0:T(8,128)(2,1)}), bf16[2048,1024]{1,0:T(8,128)(2,1)}) %all-gather.19.cloned.1.call-update) | async-done | bytes 4194320 | tf_op jit(solution)/shard_map/all_gather | solution.py:229
  664.7 14.7 fusion.485
  699.8 63.5 %reduce-scatter.36.cloned.1.call-done = bf16[512,1024]{1,0:T(8,128)(2,1)} async-done(((bf16[2048,1024]{1,0:T(8,128)(2,1)}), bf16[512,1024]{1,0:T(8,128)(2,1)}) %reduce-scatter.36.cloned.1.call-update) | async-done | bytes 1048592 | tf_op jit(solution)/shard_map/reduce_scatter | solution.py:136
  769.5 73.2 %reduce-scatter.34.cloned.1.call-done = bf16[512,1024]{1,0:T(8,128)(2,1)} async-done(((bf16[2048,1024]{1,0:T(8,128)(2,1)}), bf16[512,1024]{1,0:T(8,128)(2,1)}) %reduce-scatter.34.cloned.1.call-update) | async-done | bytes 1048592 | tf_op jit(solution)/shard_map/reduce_scatter | solution.py:127
  858.9 26.1 %all-to-all-done.2 = bf16[512,4,256]{0,2,1:T(8,128)(2,1)} async-done(((bf16[512,4,256]{0,2,1:T(8,128)(2,1)}), bf16[512,4,256]{0,2,1:T(8,128)(2,1)}, u32[]{:S(2)}, u32[]{:S(2)}) %all-to-all-start.2) | async-done | bytes 1048608 | tf_op jit(solution)/shard_map/all_to_all | solution.py:251
  949.6 15.7 bitcast_reduce_fusion.5
  965.4 16.3 fusion.159
  992.9 16.1 bitcast_reduce_fusion.4
  1009.0 15.5 fusion.183
  1032.0 75.6 %reduce-scatter.38.cloned.1.call-done = bf16[512,1024]{1,0:T(8,128)(2,1)} async-done(((bf16[2048,1024]{1,0:T(8,128)(2,1)}), bf16[512,1024]{1,0:T(8,128)(2,1)}) %reduce-scatter.38.cloned.1.call-update) | async-done | bytes 1048592 | tf_op jit(solution)/shard_map/reduce_scatter | solution.py:136
  1116.5 81.4 %all-gather.21.cloned.1.call-done = bf16[2048,1024]{1,0:T(8,128)(2,1)} async-done(((bf16[512,1024]{1,0:T(8,128)(2,1)}), bf16[2048,1024]{1,0:T(8,128)(2,1)}) %all-gather.21.cloned.1.call-update) | async-done | bytes 4194320 | tf_op jit(solution)/shard_map/all_gather | solution.py:229
  1197.8 14.5 fusion.486
  1225.8 70.3 %reduce-scatter.40.cloned.1.call-done = bf16[512,1024]{1,0:T(8,128)(2,1)} async-done(((bf16[2048,1024]{1,0:T(8,128)(2,1)}), bf16[512,1024]{1,0:T(8,128)(2,1)}) %reduce-scatter.40.cloned.1.call-update) | async-done | bytes 1048592 | tf_op jit(solution)/shard_map/reduce_scatter | solution.py:136
  1385.9 23.4 %all-to-all-done.3 = bf16[512,4,256]{0,2,1:T(8,128)(2,1)S(1)} async-done(((bf16[512,4,256]{0,2,1:T(8,128)(2,1)}), bf16[512,4,256]{0,2,1:T(8,128)(2,1)S(1)}, u32[]{:S(2)}, u32[]{:S(2)}) %all-to-all-start.3) | async-done | bytes 1048608 | tf_op jit(solution)/shard_map/all_to_all | solution.py:251
  1469.3 14.9 bitcast_reduce_fusion.1
  1484.3 14.1 bitcast_reduce_fusion
  1516.9 14.8 fusion.180
  1532.7 13.7 convolution_convert_fusion.9
  1565.6 114.9 %reduce-scatter.56.cloned.1.call-done = f32[32,4]{1,0:T(8,128)} async-done(((f32[1024,4]{1,0:T(8,128)}), f32[32,4]{1,0:T(8,128)}) %reduce-scatter.56.cloned.1.call-update) | async-done | bytes 528
  1682.0 31.3 %reduce-scatter.58.cloned.1.call-done = bf16[32,4]{1,0:T(8,128)(2,1)} async-done(((bf16[256,4]{1,0:T(8,128)(2,1)}), bf16[32,4]{1,0:T(8,128)(2,1)}) %reduce-scatter.58.cloned.1.call-update) | async-done | bytes 272
  1714.7 37.8 %reduce-scatter.60.cloned.1.call-done = bf16[128,512]{1,0:T(8,128)(2,1)} async-done(((bf16[1024,512]{1,0:T(8,128)(2,1)}), bf16[128,512]{1,0:T(8,128)(2,1)}) %reduce-scatter.60.cloned.1.call-update) | async-done | bytes 131088
  1754.3 47.8 %reduce-scatter.44.cloned.1.call-done = bf16[2,128,3,256]{3,1,2,0:T(8,128)(2,1)} async-done(((bf16[2,1024,3,256]{3,1,2,0:T(8,128)(2,1)}), bf16[2,128,3,256]{3,1,2,0:T(8,128)(2,1)}) %reduce-scatter.44.cloned.1.call-update) | async-done | bytes 393232 | tf_op jit(solution)/shard_map/reduce_scatter | solution.py:292
  1804.1 77.2 %reduce-scatter.42.cloned.1.call-done = bf16[512,1024]{1,0:T(8,128)(2,1)} async-done(((bf16[2048,1024]{1,0:T(8,128)(2,1)}), bf16[512,1024]{1,0:T(8,128)(2,1)}) %reduce-scatter.42.cloned.1.call-update) | async-done | bytes 1048592 | tf_op jit(solution)/shard_map/reduce_scatter | solution.py:136
  1897.2 127.1 %reduce-scatter.52.cloned.1.call-done = f32[32,4]{1,0:T(8,128)} async-done(((f32[1024,4]{1,0:T(8,128)}), f32[32,4]{1,0:T(8,128)}) %reduce-scatter.52.cloned.1.call-update) | async-done | bytes 528
  2025.8 131.3 %reduce-scatter.54.cloned.1.call-done = f32[32,4]{1,0:T(8,128)} async-done(((f32[1024,4]{1,0:T(8,128)}), f32[32,4]{1,0:T(8,128)}) %reduce-scatter.54.cloned.1.call-update) | async-done | bytes 528
  (612 shorter events, 505.9 us)
Async XLA Ops:
  7.2 89.6 %all-gather.11.cloned.1.call-start = ((), (), s32[]{:S(2)}) async-start(), calls=%async_computation.21 | async-start | bytes 5242880 | tf_op jit(solution)/shard_map/all_gather | solution.py:123
  11.8 333.9 %copy-start.87 = (f32[1,1,1024]{2,1,0:T(1,128)}, f32[1,1,1024]{2,1,0:T(1,128)S(1)}, u32[]{:S(2)}) copy-start(f32[1,1,1024]{2,1,0:T(1,128)S(1)} %get-tuple-element.293) | copy-start | bytes 12292
  13.2 148.1 %all-gather.23.cloned.1.call-start = ((), (), s32[]{:S(2)}) async-start(), calls=%async_computation.37 | async-start | bytes 2621440 | tf_op jit(solution)/shard_map/all_gather | solution.py:180
  122.8 42.7 %all-to-all-start = ((bf16[4,512,256]{1,2,0:T(8,128)(2,1)}), bf16[4,512,256]{1,2,0:T(8,128)(2,1)S(1)}, u32[]{:S(2)}, u32[]{:S(2)}) async-start(bf16[4,512,256]{1,2,0:T(8,128)(2,1)} %copy.171), calls=%async_computation | async-start | bytes 2097152 | tf_op jit(solution)/shard_map/all_to_all | solution.py:181
  126.4 124.5 %all-gather.13.cloned.1.call-start = ((), (), s32[]{:S(2)}) async-start(), calls=%async_computation.22 | async-start | bytes 5242880 | tf_op jit(solution)/shard_map/all_gather | solution.py:123
  171.3 172.3 %reduce-scatter.32.cloned.1.call-start = ((), (), s32[]{:S(2)}) async-start(), calls=%async_computation.23 | async-start | bytes 5242880 | tf_op jit(solution)/shard_map/reduce_scatter | solution.py:127
  268.2 161.2 %all-gather.15.cloned.1.call-start = ((), (), s32[]{:S(2)}) async-start(), calls=%async_computation.24 | async-start | bytes 5242880 | tf_op jit(solution)/shard_map/all_gather | solution.py:123
  347.9 137.3 %all-gather.25.cloned.1.call-start = ((), (), s32[]{:S(2)}) async-start(), calls=%async_computation.38 | async-start | bytes 2621440 | tf_op jit(solution)/shard_map/all_gather | solution.py:180
  459.0 38.7 %all-to-all-start.1 = ((bf16[4,512,256]{1,2,0:T(8,128)(2,1)}), bf16[4,512,256]{1,2,0:T(8,128)(2,1)}, u32[]{:S(2)}, u32[]{:S(2)}) async-start(bf16[4,512,256]{1,2,0:T(8,128)(2,1)} %copy.182), calls=%async_computation.2 | async-start | bytes 2097152 | tf_op jit(solution)/shard_map/all_to_all | solution.py:181
  463.3 119.9 %all-gather.17.cloned.1.call-start = ((), (), s32[]{:S(2)}) async-start(), calls=%async_computation.25 | async-start | bytes 5242880 | tf_op jit(solution)/shard_map/all_gather | solution.py:123
  503.7 161.0 %all-gather.19.cloned.1.call-start = ((), (), s32[]{:S(2)}) async-start(), calls=%async_computation.27 | async-start | bytes 5242880 | tf_op jit(solution)/shard_map/all_gather | solution.py:229
  507.8 255.4 %reduce-scatter.36.cloned.1.call-start = ((), (), s32[]{:S(2)}) async-start(), calls=%async_computation.28 | async-start | bytes 5242880 | tf_op jit(solution)/shard_map/reduce_scatter | solution.py:136
  687.8 154.9 %reduce-scatter.34.cloned.1.call-start = ((), (), s32[]{:S(2)}) async-start(), calls=%async_computation.26 | async-start | bytes 5242880 | tf_op jit(solution)/shard_map/reduce_scatter | solution.py:127
  854.3 30.7 %all-to-all-start.2 = ((bf16[512,4,256]{0,2,1:T(8,128)(2,1)}), bf16[512,4,256]{0,2,1:T(8,128)(2,1)}, u32[]{:S(2)}, u32[]{:S(2)}) async-start(bf16[512,4,256]{0,2,1:T(8,128)(2,1)} %bitcast.431), calls=%async_computation.5 | async-start | bytes 2097152 | tf_op jit(solution)/shard_map/all_to_all | solution.py:251
  858.5 249.1 %reduce-scatter.38.cloned.1.call-start = ((), (), s32[]{:S(2)}) async-start(), calls=%async_computation.29 | async-start | bytes 5242880 | tf_op jit(solution)/shard_map/reduce_scatter | solution.py:136
  1032.0 165.9 %all-gather.21.cloned.1.call-start = ((), (), s32[]{:S(2)}) async-start(), calls=%async_computation.30 | async-start | bytes 5242880 | tf_op jit(solution)/shard_map/all_gather | solution.py:229
  1116.4 179.7 %reduce-scatter.40.cloned.1.call-start = ((), (), s32[]{:S(2)}) async-start(), calls=%async_computation.31 | async-start | bytes 5242880 | tf_op jit(solution)/shard_map/reduce_scatter | solution.py:136
  1220.7 278.7 %reduce-scatter.48.cloned.1.call-start = ((), (), s32[]{:S(2)}) async-start(), calls=%async_computation.35 | async-start | bytes 2621440 | tf_op jit(solution)/shard_map/reduce_scatter | solution.py:244
  1225.5 274.0 %reduce-scatter.46.cloned.1.call-start = ((), (), s32[]{:S(2)}) async-start(), calls=%async_computation.34 | async-start | bytes 2621440 | tf_op jit(solution)/shard_map/reduce_scatter | solution.py:244
  1305.2 253.9 %reduce-scatter.62.cloned.1.call-start = ((), (), s32[]{:S(2)}) async-start(), calls=%async_computation.44 | async-start | bytes 294912
  1316.8 243.7 %reduce-scatter.64.cloned.1.call-start = ((), (), s32[]{:S(2)}) async-start(), calls=%async_computation.45 | async-start | bytes 4718592
  1347.3 216.3 %reduce-scatter.50.cloned.1.call-start = ((), (), s32[]{:S(2)}) async-start(), calls=%async_computation.36 | async-start | bytes 4718592 | tf_op jit(solution)/shard_map/reduce_scatter | solution.py:301
  1369.2 40.2 %all-to-all-start.3 = ((bf16[512,4,256]{0,2,1:T(8,128)(2,1)}), bf16[512,4,256]{0,2,1:T(8,128)(2,1)S(1)}, u32[]{:S(2)}, u32[]{:S(2)}) async-start(bf16[512,4,256]{0,2,1:T(8,128)(2,1)} %bitcast.88), calls=%async_computation.8 | async-start | bytes 2097152 | tf_op jit(solution)/shard_map/all_to_all | solution.py:251
  1373.3 307.2 %reduce-scatter.56.cloned.1.call-start = ((), (), s32[]{:S(2)}) async-start(), calls=%async_computation.41 | async-start | bytes 540672
  1385.5 327.8 %reduce-scatter.58.cloned.1.call-start = ((), (), s32[]{:S(2)}) async-start(), calls=%async_computation.42 | async-start | bytes 73728
  1499.4 253.1 %reduce-scatter.60.cloned.1.call-start = ((), (), s32[]{:S(2)}) async-start(), calls=%async_computation.43 | async-start | bytes 1179648
  1503.2 298.9 %reduce-scatter.44.cloned.1.call-start = ((), (), s32[]{:S(2)}) async-start(), calls=%async_computation.33 | async-start | bytes 3538944 | tf_op jit(solution)/shard_map/reduce_scatter | solution.py:292
  1550.2 331.1 %reduce-scatter.42.cloned.1.call-start = ((), (), s32[]{:S(2)}) async-start(), calls=%async_computation.32 | async-start | bytes 5242880 | tf_op jit(solution)/shard_map/reduce_scatter | solution.py:136
  1558.3 323.0 %copy-start.5 = (f32[512,1024]{1,0:T(8,128)S(1)}, f32[512,1024]{1,0:T(8,128)}, u32[]{:S(2)}) copy-start(f32[512,1024]{1,0:T(8,128)} %param.52) | copy-start | bytes 6291460
  1558.4 322.9 %copy-start.90 = (f32[1,1,1024]{2,1,0:T(1,128)S(1)}, f32[1,1,1024]{2,1,0:T(1,128)}, u32[]{:S(2)}) copy-start(f32[1,1,1024]{2,1,0:T(1,128)} %copy-done.89) | copy-start | bytes 12292
  1558.4 465.9 %reduce-scatter.52.cloned.1.call-start = ((), (), s32[]{:S(2)}) async-start(), calls=%async_computation.39 | async-start | bytes 540672
  1889.6 267.5 %reduce-scatter.54.cloned.1.call-start = ((), (), s32[]{:S(2)}) async-start(), calls=%async_computation.40 | async-start | bytes 540672
  (157 other events, 3773.0 us)
Sparse Core Ops, SparseCore 0:
  13.3 83.4 all-gather.10
  99.0 62.3 all-gather.22
  171.4 79.4 all-gather.12
  268.3 75.2 reduce-scatter.31
  348.1 81.2 all-gather.14
  430.9 54.3 all-gather.24
  503.8 79.2 all-gather.16
  585.4 79.2 all-gather.18
  687.9 75.2 reduce-scatter.35
  765.4 77.2 reduce-scatter.33
  1032.1 75.4 reduce-scatter.37
  1116.5 81.2 all-gather.20
  1220.8 75.2 reduce-scatter.39
  1298.4 44.3 reduce-scatter.47
  1344.9 52.0 reduce-scatter.45
  1400.2 34.4 reduce-scatter.61
  1437.9 51.3 reduce-scatter.63
  1492.9 51.2 reduce-scatter.49
  1546.4 134.0 reduce-scatter.55
  1683.6 29.5 reduce-scatter.57
  1716.4 36.0 reduce-scatter.59
  1755.9 46.1 reduce-scatter.43
  1804.5 76.7 reduce-scatter.41
  1889.7 134.5 reduce-scatter.51
  2026.7 130.3 reduce-scatter.53
where the time goes:
time: 2180 us; the launch traced here: 2170 us
  waiting for transfers between devices  1510 us (69%)
  matrix products  445 us (20%)
  local copies, waits for them, and re-layouts  97.3 us (4%)
  other arithmetic  77 us (4%)
    unnamed x32, waiting for transfers between devices  443 us
    all_gather x4, waiting for transfers between devices, gather_normed(): return lax.all_gather(normed, 'tensor', axis=0, tiled=True)  309 us
    reduce_scatter x4, waiting for transfers between devices, input_sum(): lax.psum_scatter(contract_cols(grads, weight).astype(jnp.bfloat16), 'tens...  287 us
    all_gather x2, waiting for transfers between devices, on_device(): grad_full = lax.all_gather(grad_low, 'tensor', axis=0, tiled=True)  152 us
    reduce_scatter x2, waiting for transfers between devices, feed_sum(): lax.psum_scatter(jnp.dot(active, weight, preferred_element_type=jnp.float...  148 us
    dot_general x8, matrix products, attend_backward(): jnp.einsum('hqk,khd->qhd', grad_scores, key_rows[:row_stop], preferred_el...  96.4 us
    dot_general x8, matrix products, attend_backward(): jnp.einsum('hqk,qhd->khd', grad_scores, q_rows, preferred_element_type=jn...  93.8 us
    unnamed x352, local copies, waits for them, and re-layouts  65.6 us
  transfers between devices with their start and end apart: 29, of which 24 were waited for; matrix products, arithmetic and copies ran while one was open for 16% of the time, Pallas kernels for 0%

commit v1 on v0

--- a/solution.py
+++ b/solution.py
@@ -1,11 +1,17 @@
+import functools
+
 import jax
 import jax.numpy as jnp
 from jax import lax
+from jax.experimental import pallas as pl
+from jax.experimental.pallas import tpu as pltpu
 from jax.sharding import PartitionSpec as P
 
 D = 1024
 HEAD = 128
 LAYERS = 2
+LOG2E = 1.4426950408889634
+VMEM_LIMIT = 56 * 1024 * 1024
 
 
 EPS = 1e-05
@@ -30,93 +36,114 @@
     )
 
 
-def segment_ids(lengths_row, tokens):
+def doc_starts(lengths_row, tokens):
     doc_ends = jnp.cumsum(lengths_row)
     positions = jnp.arange(tokens, dtype=jnp.int32)
-    return jnp.sum((positions[:, None] >= doc_ends[None, :]).astype(jnp.int32), 1)
-
-
-def block_mask(seg_ids, row_start, row_stop):
-    positions = jnp.arange(row_stop, dtype=jnp.int32)
-    row_ids = positions[row_start:row_stop]
-    same_doc = seg_ids[row_start:row_stop, None] == seg_ids[None, :row_stop]
-    return same_doc & (positions[None, :] <= row_ids[:, None])
-
-
-def attend_forward(queries, key_rows, value_rows, seg_ids):
-    tokens = queries.shape[0]
-    block_len = min(512, tokens)
-    score_scale = float(HEAD) ** (-0.5)
-    outputs_list = []
-    sums_list = []
-    for block_id in range(tokens // block_len):
-        row_start = block_id * block_len
-        row_stop = row_start + block_len
-        scores = (
-            jnp.einsum(
-                "qhd,khd->hqk",
-                queries[row_start:row_stop],
-                key_rows[:row_stop],
-                preferred_element_type=jnp.float32,
-            )
-            * score_scale
-        )
-        scores = jnp.where(block_mask(seg_ids, row_start, row_stop)[None], scores, NEG)
-        largest = jnp.max(scores, -1, keepdims=True)
-        expo = jnp.exp(scores - largest)
-        totals = jnp.sum(expo, -1, keepdims=True)
-        weights = (expo / totals).astype(jnp.bfloat16)
-        outputs_list.append(
-            jnp.einsum(
-                "hqk,khd->qhd", weights, value_rows[:row_stop], preferred_element_type=jnp.float32
-            )
-        )
-        sums_list.append((largest + jnp.log(totals))[..., 0])
-    return (jnp.concatenate(outputs_list, 0), jnp.concatenate(sums_list, 1))
-
-
-def attend_backward(queries, key_rows, value_rows, seg_ids, log_sums, grad_out):
-    tokens = queries.shape[0]
-    block_len = min(512, tokens)
-    score_scale = float(HEAD) ** (-0.5)
-    grad_keys = jnp.zeros(key_rows.shape, jnp.float32)
-    grad_values = jnp.zeros(value_rows.shape, jnp.float32)
-    grad_queries = []
-    for block_id in range(tokens // block_len):
-        row_start = block_id * block_len
-        row_stop = row_start + block_len
-        q_rows = queries[row_start:row_stop]
-        out_rows = grad_out[row_start:row_stop]
-        scores = (
-            jnp.einsum(
-                "qhd,khd->hqk", q_rows, key_rows[:row_stop], preferred_element_type=jnp.float32
-            )
-            * score_scale
-        )
-        scores = jnp.where(block_mask(seg_ids, row_start, row_stop)[None], scores, NEG)
-        probs = jnp.exp(scores - log_sums[:, row_start:row_stop, None])
-        grad_probs = jnp.einsum(
-            "qhd,khd->hqk", out_rows, value_rows[:row_stop], preferred_element_type=jnp.float32
-        )
-        inner_sum = jnp.sum(probs * grad_probs, -1, keepdims=True)
-        grad_scores = (probs * (grad_probs - inner_sum) * score_scale).astype(jnp.bfloat16)
-        grad_queries.append(
-            jnp.einsum(
-                "hqk,khd->qhd", grad_scores, key_rows[:row_stop], preferred_element_type=jnp.float32
-            )
-        )
-        grad_keys = grad_keys.at[:row_stop].add(
-            jnp.einsum("hqk,qhd->khd", grad_scores, q_rows, preferred_element_type=jnp.float32)
-        )
-        grad_values = grad_values.at[:row_stop].add(
-            jnp.einsum(
-                "hqk,qhd->khd",
-                probs.astype(jnp.bfloat16),
-                out_rows,
-                preferred_element_type=jnp.float32,
-            )
-        )
-    return (jnp.concatenate(grad_queries, 0), grad_keys, grad_values)
+    return jnp.max(jnp.where(positions[:, None] >= doc_ends[None, :], doc_ends[None, :], 0), 1)[None]
+
+def dot_nt(a,b):
+    return lax.dot_general(a,b,(((1,),(1,)),((),())),preferred_element_type=jnp.float32)
+def dot_nn(a,b):
+    return lax.dot_general(a,b,(((1,),(0,)),((),())),preferred_element_type=jnp.float32)
+
+def attn_fwd_kernel(block, starts_ref, q_ref, k_ref, v_ref, o_ref, p_ref, s_scr):
+    tokens=q_ref.shape[0]
+    factor=float(HEAD)**-0.5*LOG2E
+    vt=v_ref[...].T
+    for i in range(tokens//block):
+        qi=q_ref[i*block:(i+1)*block,:]
+        start_row=starts_ref[0:1,i*block:(i+1)*block]
+        base=i*(i+1)//2*block
+        peak=None
+        for j in range(i+1):
+            s=dot_nt(k_ref[j*block:(j+1)*block,:],qi)*factor
+            key_ids=j*block+lax.broadcasted_iota(jnp.int32,(block,block),0)
+            ok=key_ids>=start_row
+            if j==i:
+                ok=ok&(key_ids<=i*block+lax.broadcasted_iota(jnp.int32,(block,block),1))
+            s=jnp.where(ok,s,NEG)
+            s_scr[j*block:(j+1)*block,:]=s
+            top=jnp.max(s,0,keepdims=True)
+            peak=top if peak is None else jnp.maximum(peak,top)
+        total=None
+        for j in range(i+1):
+            e=jnp.exp2(s_scr[j*block:(j+1)*block,:]-peak)
+            s_scr[j*block:(j+1)*block,:]=e
+            part=jnp.sum(e,0,keepdims=True)
+            total=part if total is None else total+part
+        inv=1.0/total
+        acc=None
+        for j in range(i+1):
+            p=(s_scr[j*block:(j+1)*block,:]*inv).astype(jnp.bfloat16)
+            p_ref[0,base+j*block:base+(j+1)*block,:]=p
+            part=dot_nn(vt[:,j*block:(j+1)*block],p)
+            acc=part if acc is None else acc+part
+        o_ref[i*block:(i+1)*block,:]=acc.T.astype(jnp.bfloat16)
+
+def attn_fwd(q,k,v,starts):
+    tokens,inner=q.shape
+    heads=inner//HEAD
+    block=min(512,tokens)
+    nb=tokens//block
+    packed=nb*(nb+1)//2*block
+    spec=pl.BlockSpec((tokens,HEAD),lambda h:(0,h))
+    return pl.pallas_call(
+        functools.partial(attn_fwd_kernel,block),
+        grid=(heads,),
+        in_specs=[pl.BlockSpec((1,tokens),lambda h:(0,0)),spec,spec,spec],
+        out_specs=[spec,pl.BlockSpec((1,packed,block),lambda h:(h,0,0))],
+        out_shape=[jax.ShapeDtypeStruct((tokens,inner),jnp.bfloat16),jax.ShapeDtypeStruct((heads,packed,block),jnp.bfloat16)],
+        scratch_shapes=[pltpu.VMEM((tokens,block),jnp.float32)],
+        compiler_params=pltpu.CompilerParams(vmem_limit_bytes=VMEM_LIMIT),
+    )(starts,q,k,v)
+
+def attn_bwd_kernel(block,q_ref,k_ref,v_ref,o_ref,do_ref,p_ref,dq_ref,dk_ref,dv_ref,dk_acc,dv_acc):
+    tokens=q_ref.shape[0]
+    scale=float(HEAD)**-0.5
+    kt=k_ref[...].T
+    for i in range(tokens//block):
+        rows=slice(i*block,(i+1)*block)
+        qi=q_ref[rows,:]
+        doi=do_ref[rows,:]
+        prod=doi.astype(jnp.float32)*o_ref[rows,:].astype(jnp.float32)
+        inner=jnp.sum(prod.T,0,keepdims=True)
+        base=i*(i+1)//2*block
+        acc=None
+        for j in range(i+1):
+            cols=slice(j*block,(j+1)*block)
+            p=p_ref[0,base+j*block:base+(j+1)*block,:]
+            dp=dot_nt(v_ref[cols,:],doi)
+            ds=(p.astype(jnp.float32)*(dp-inner)).astype(jnp.bfloat16)
+            dv=dot_nn(p,doi)
+            dk=dot_nn(ds,qi)
+            if i==j:
+                dv_acc[cols,:]=dv
+                dk_acc[cols,:]=dk
+            else:
+                dv_acc[cols,:]+=dv
+                dk_acc[cols,:]+=dk
+            part=dot_nn(kt[:,cols],ds)
+            acc=part if acc is None else acc+part
+        dq_ref[rows,:]=(acc*scale).T.astype(jnp.bfloat16)
+    dk_ref[...]=(dk_acc[...]*scale).astype(jnp.bfloat16)
+    dv_ref[...]=dv_acc[...].astype(jnp.bfloat16)
+
+def attn_bwd(q,k,v,o,do,p):
+    tokens,inner=q.shape
+    heads=inner//HEAD
+    block=min(512,tokens)
+    packed=p.shape[1]
+    spec=pl.BlockSpec((tokens,HEAD),lambda h:(0,h))
+    shape=jax.ShapeDtypeStruct((tokens,inner),jnp.bfloat16)
+    return pl.pallas_call(
+        functools.partial(attn_bwd_kernel,block),
+        grid=(heads,),
+        in_specs=[spec]*5+[pl.BlockSpec((1,packed,block),lambda h:(h,0,0))],
+        out_specs=[spec]*3,
+        out_shape=[shape]*3,
+        scratch_shapes=[pltpu.VMEM((tokens,HEAD),jnp.float32)]*2,
+        compiler_params=pltpu.CompilerParams(vmem_limit_bytes=VMEM_LIMIT),
+    )(q,k,v,o,do,p)
 
 
 def gather_normed(normed):
@@ -155,9 +182,7 @@
     dev_rows = inputs.shape[0]
     tokens = dev_rows * lax.axis_size("tensor")
     inner = qv_bias.shape[2]
-    local_heads = inner // HEAD
-    head_shape = (tokens, local_heads, HEAD)
-    seg_ids = segment_ids(lengths[0], tokens)
+    starts = doc_starts(lengths[0], tokens)
     stream = inputs
     kept = []
     for layer_id in range(LAYERS):
@@ -166,17 +191,10 @@
         projected = jnp.dot(
             full_one, w_qkv[layer_id].reshape(D, 3 * inner), preferred_element_type=jnp.float32
         )
-        queries = (
-            (projected[:, :inner] + qv_bias[layer_id, 0]).astype(jnp.bfloat16).reshape(head_shape)
-        )
-        key_rows = projected[:, inner : 2 * inner].astype(jnp.bfloat16).reshape(head_shape)
-        value_rows = (
-            (projected[:, 2 * inner :] + qv_bias[layer_id, 1])
-            .astype(jnp.bfloat16)
-            .reshape(head_shape)
-        )
-        attended, log_sums = attend_forward(queries, key_rows, value_rows, seg_ids)
-        attended = attended.reshape(tokens, inner).astype(jnp.bfloat16)
+        queries = (projected[:, :inner] + qv_bias[layer_id, 0]).astype(jnp.bfloat16)
+        key_rows = projected[:, inner : 2 * inner].astype(jnp.bfloat16)
+        value_rows = (projected[:, 2 * inner :] + qv_bias[layer_id, 1]).astype(jnp.bfloat16)
+        attended, probs = attn_fwd(queries, key_rows, value_rows, starts)
         out_full = lax.all_gather(w_out[layer_id], "tensor", axis=0, tiled=True)
         head_rows = lax.all_to_all(attended, "tensor", split_axis=0, concat_axis=1, tiled=True)
         branch = jnp.dot(head_rows, out_full, preferred_element_type=jnp.float32)
@@ -197,7 +215,8 @@
                 queries,
                 key_rows,
                 value_rows,
-                log_sums,
+                probs,
+                attended,
                 head_rows,
                 out_full,
                 middle,
@@ -216,7 +235,8 @@
             queries,
             key_rows,
             value_rows,
-            log_sums,
+            probs,
+            attended,
             head_rows,
             out_full,
             middle,
@@ -251,12 +271,9 @@
         grad_attended = lax.all_to_all(
             grad_heads, "tensor", split_axis=1, concat_axis=0, tiled=True
         )
-        grad_q, grad_k, grad_v = attend_backward(
-            queries, key_rows, value_rows, seg_ids, log_sums, grad_attended.reshape(head_shape)
-        )
-        low_q = grad_q.astype(jnp.bfloat16).reshape(tokens, inner)
-        low_k = grad_k.astype(jnp.bfloat16).reshape(tokens, inner)
-        low_v = grad_v.astype(jnp.bfloat16).reshape(tokens, inner)
+        low_q, low_k, low_v = attn_bwd(
+            queries, key_rows, value_rows, attended, grad_attended, probs
+        )
         grad_mixed = jnp.concatenate([low_q, low_k, low_v], 1)
         grad_qkv_w = contract_rows(full_one, grad_mixed).reshape(D, 3, inner)
         grad_qv = jnp.stack(

time: 2180 us -> 2040 us (0.936)
  matrix products: 445 us -> 169 us
  waiting for transfers between devices: 1510 us -> 1600 us
  Pallas kernels: 0 us -> 56.1 us
  blocking collectives: 0 us -> 30.3 us
    dot_general x48 -> x0, matrix products: 266 us -> none  [the longest x8 96.4 us: attend_backward(): jnp.einsum('hqk,khd->qhd', grad_scores, key_rows[:row_stop], preferred_el...]
    pallas_call x0 -> x4, Pallas kernels: none -> 56.1 us  [the longest x2 29.4 us: attn_bwd(): pl.pallas_call(functools.partial(attn_bwd_kernel, block), grid=(heads,),...]
    reduce_scatter x1, waiting for transfers between devices: 0.01 us -> 51.9 us  [on_device(): lax.psum_scatter(up_all.astype(jnp.bfloat16), 'dp', scatter_dimension=1,...]
    unnamed x32, waiting for transfers between devices: 443 us -> 491 us
    all_to_all x0 -> x1, blocking collectives: none -> 30.3 us  [on_device(): lax.all_to_all(grad_heads, 'tensor', split_axis=1, concat_axis=0, tiled=T...]
    all_to_all x2 -> x1, waiting for transfers between devices: 49.5 us -> 34.5 us  [on_device(): lax.all_to_all(grad_heads, 'tensor', split_axis=1, concat_axis=0, tiled=T...]
    unnamed x352 -> x160, local copies, waits for them, and re-layouts: 65.6 us -> 65.6 us
  transfers between devices with their start and end apart: 29 -> 28, of which waited for: 24 -> 25; matrix products, arithmetic and copies ran while one was open for 16% -> 9% of each run, Pallas kernels for 0% -> 2%
where the time goes in v1:
time: 2040 us; the launch traced here: 2030 us
  waiting for transfers between devices  1600 us (78%)
  matrix products  169 us (8%)
  local copies, waits for them, and re-layouts  80.5 us (4%)
  other arithmetic  64.4 us (3%)
  Pallas kernels  56.1 us (3%)
  blocking collectives  30.3 us (1%)
  starting transfers between devices  22.9 us (1%)
    unnamed x32, waiting for transfers between devices  491 us
    all_gather x4, waiting for transfers between devices, gather_normed(): return lax.all_gather(normed, 'tensor', axis=0, tiled=True)  302 us
    reduce_scatter x4, waiting for transfers between devices, input_sum(): lax.psum_scatter(contract_cols(grads, weight).astype(jnp.bfloat16), 'tens...  286 us
    all_gather x2, waiting for transfers between devices, on_device(): grad_full = lax.all_gather(grad_low, 'tensor', axis=0, tiled=True)  151 us
    reduce_scatter x2, waiting for transfers between devices, feed_sum(): lax.psum_scatter(jnp.dot(active, weight, preferred_element_type=jnp.float...  150 us
    all_gather x2, waiting for transfers between devices, on_device(): out_full = lax.all_gather(w_out[layer_id], 'tensor', axis=0, tiled=True)  75.4 us
    unnamed x160, local copies, waits for them, and re-layouts  65.6 us
    dot_general x8, matrix products, contract_cols(): lax.dot_general(left, right, (((1,), (1,)), ((), ())), preferred_element_...  57.2 us
  transfers between devices with their start and end apart: 28, of which 25 were waited for; matrix products, arithmetic and copies ran while one was open for 9% of the time, Pallas kernels for 2%

profile of v1, /device:TPU:0, one launch (start us, length us, event | category | flops | bytes accessed | tf_op | source)
XLA Modules:
  0.0 2034.1 jit_solution(14164958427289956651)
XLA Ops:
  18.0 77.4 %all-gather.11.cloned.1.call-done = bf16[2048,1024]{1,0:T(8,128)(2,1)} async-done(((bf16[512,1024]{1,0:T(8,128)(2,1)}), bf16[2048,1024]{1,0:T(8,128)(2,1)}) %all-gather.11.cloned.1.call-update) | async-done | bytes 4194320 | tf_op jit(solution)/shard_map/all_gather | solution.py:150
  103.5 13.4 shard_map.203
  122.7 37.5 %all-gather.23.cloned.1.call-done = bf16[1,1024,1024]{2,1,0:T(8,128)(2,1)} async-done(((bf16[1,256,1024]{2,1,0:T(8,128)(2,1)}), bf16[1,1024,1024]{2,1,0:T(8,128)(2,1)}) %all-gather.23.cloned.1.call-update) | async-done | bytes 2097168 | tf_op jit(solution)/shard_map/all_gather | solution.py:198
  169.6 79.3 %all-gather.13.cloned.1.call-done = bf16[2048,1024]{1,0:T(8,128)(2,1)} async-done(((bf16[512,1024]{1,0:T(8,128)(2,1)}), bf16[2048,1024]{1,0:T(8,128)(2,1)}) %all-gather.13.cloned.1.call-update) | async-done | bytes 4194320 | tf_op jit(solution)/shard_map/all_gather | solution.py:150
  266.2 75.4 %reduce-scatter.32.cloned.1.call-done = bf16[512,1024]{1,0:T(8,128)(2,1)} async-done(((bf16[2048,1024]{1,0:T(8,128)(2,1)}), bf16[512,1024]{1,0:T(8,128)(2,1)}) %reduce-scatter.32.cloned.1.call-update) | async-done | bytes 1048592 | tf_op jit(solution)/shard_map/reduce_scatter | solution.py:154
  349.2 78.2 %all-gather.15.cloned.1.call-done = bf16[2048,1024]{1,0:T(8,128)(2,1)} async-done(((bf16[512,1024]{1,0:T(8,128)(2,1)}), bf16[2048,1024]{1,0:T(8,128)(2,1)}) %all-gather.15.cloned.1.call-update) | async-done | bytes 4194320 | tf_op jit(solution)/shard_map/all_gather | solution.py:150
  435.9 13.3 shard_map.204
  455.0 37.9 %all-gather.25.cloned.1.call-done = bf16[1,1024,1024]{2,1,0:T(8,128)(2,1)} async-done(((bf16[1,256,1024]{2,1,0:T(8,128)(2,1)}), bf16[1,1024,1024]{2,1,0:T(8,128)(2,1)}) %all-gather.25.cloned.1.call-update) | async-done | bytes 2097168 | tf_op jit(solution)/shard_map/all_gather | solution.py:198
  515.5 66.9 %all-gather.17.cloned.1.call-done = bf16[2048,1024]{1,0:T(8,128)(2,1)} async-done(((bf16[512,1024]{1,0:T(8,128)(2,1)}), bf16[2048,1024]{1,0:T(8,128)(2,1)}) %all-gather.17.cloned.1.call-update) | async-done | bytes 4194320 | tf_op jit(solution)/shard_map/all_gather | solution.py:150
  593.2 70.2 %all-gather.19.cloned.1.call-done = bf16[2048,1024]{1,0:T(8,128)(2,1)} async-done(((bf16[512,1024]{1,0:T(8,128)(2,1)}), bf16[2048,1024]{1,0:T(8,128)(2,1)}) %all-gather.19.cloned.1.call-update) | async-done | bytes 4194320 | tf_op jit(solution)/shard_map/all_gather | solution.py:249
  663.3 14.3 fusion.106
  686.3 11.8 convolution_convert_fusion.4
  698.1 63.4 %reduce-scatter.36.cloned.1.call-done = bf16[512,1024]{1,0:T(8,128)(2,1)} async-done(((bf16[2048,1024]{1,0:T(8,128)(2,1)}), bf16[512,1024]{1,0:T(8,128)(2,1)}) %reduce-scatter.36.cloned.1.call-update) | async-done | bytes 1048592 | tf_op jit(solution)/shard_map/reduce_scatter | solution.py:163
  766.4 74.5 %reduce-scatter.34.cloned.1.call-done = bf16[512,1024]{1,0:T(8,128)(2,1)} async-done(((bf16[2048,1024]{1,0:T(8,128)(2,1)}), bf16[512,1024]{1,0:T(8,128)(2,1)}) %reduce-scatter.34.cloned.1.call-update) | async-done | bytes 1048592 | tf_op jit(solution)/shard_map/reduce_scatter | solution.py:154
  847.2 30.3 %all_to_all.76 = bf16[512,4,256]{2,0,1:T(8,128)(2,1)} all-to-all(bf16[512,4,256]{2,0,1:T(8,128)(2,1)S(1)} %bitcast.184), channel_id=1, replica_groups=mesh['dp'=8,'tensor'=4] {'tensor'}, dimensions={1} | all-to-all | bytes 2097152 | tf_op jit(solution)/shard_map/all_to_all | solution.py:271
  877.4 14.7 shard_map.205
  901.1 75.9 %reduce-scatter.38.cloned.1.call-done = bf16[512,1024]{1,0:T(8,128)(2,1)} async-done(((bf16[2048,1024]{1,0:T(8,128)(2,1)}), bf16[512,1024]{1,0:T(8,128)(2,1)}) %reduce-scatter.38.cloned.1.call-update) | async-done | bytes 1048592 | tf_op jit(solution)/shard_map/reduce_scatter | solution.py:163
  984.8 81.2 %all-gather.21.cloned.1.call-done = bf16[2048,1024]{1,0:T(8,128)(2,1)} async-done(((bf16[512,1024]{1,0:T(8,128)(2,1)}), bf16[2048,1024]{1,0:T(8,128)(2,1)}) %all-gather.21.cloned.1.call-update) | async-done | bytes 4194320 | tf_op jit(solution)/shard_map/all_gather | solution.py:249
  1066.0 14.2 fusion.107
  1094.2 69.7 %reduce-scatter.40.cloned.1.call-done = bf16[512,1024]{1,0:T(8,128)(2,1)} async-done(((bf16[2048,1024]{1,0:T(8,128)(2,1)}), bf16[512,1024]{1,0:T(8,128)(2,1)}) %reduce-scatter.40.cloned.1.call-update) | async-done | bytes 1048592 | tf_op jit(solution)/shard_map/reduce_scatter | solution.py:163
  1197.4 11.3 copy.63
  1242.7 34.5 %all-to-all-done.3 = bf16[512,4,256]{2,0,1:T(8,128)(2,1)S(1)} async-done(((bf16[512,4,256]{2,0,1:T(8,128)(2,1)}), bf16[512,4,256]{2,0,1:T(8,128)(2,1)S(1)}, u32[]{:S(2)}, u32[]{:S(2)}) %all-to-all-start.3) | async-done | bytes 1048608 | tf_op jit(solution)/shard_map/all_to_all | solution.py:271
  1278.2 14.7 shard_map.206
  1330.9 27.4 %reduce-scatter.64.cloned.1.call-done = bf16[128,2048]{1,0:T(8,128)(2,1)} async-done(((bf16[1024,2048]{1,0:T(8,128)(2,1)}), bf16[128,2048]{1,0:T(8,128)(2,1)}) %reduce-scatter.64.cloned.1.call-update) | async-done | bytes 524304
  1361.3 51.9 %reduce-scatter.50.cloned.1.call-done = bf16[2,128,1024]{2,1,0:T(8,128)(2,1)} async-done(((bf16[2,1024,1024]{2,1,0:T(8,128)(2,1)}), bf16[2,128,1024]{2,1,0:T(8,128)(2,1)}) %reduce-scatter.50.cloned.1.call-update) | async-done | bytes 524304 | tf_op jit(solution)/shard_map/reduce_scatter | solution.py:318
  1415.4 134.8 %reduce-scatter.56.cloned.1.call-done = f32[32,4]{1,0:T(8,128)} async-done(((f32[1024,4]{1,0:T(8,128)}), f32[32,4]{1,0:T(8,128)}) %reduce-scatter.56.cloned.1.call-update) | async-done | bytes 528
  1551.6 31.2 %reduce-scatter.58.cloned.1.call-done = bf16[32,4]{1,0:T(8,128)(2,1)} async-done(((bf16[256,4]{1,0:T(8,128)(2,1)}), bf16[32,4]{1,0:T(8,128)(2,1)}) %reduce-scatter.58.cloned.1.call-update) | async-done | bytes 272
  1584.3 37.8 %reduce-scatter.60.cloned.1.call-done = bf16[128,512]{1,0:T(8,128)(2,1)} async-done(((bf16[1024,512]{1,0:T(8,128)(2,1)}), bf16[128,512]{1,0:T(8,128)(2,1)}) %reduce-scatter.60.cloned.1.call-update) | async-done | bytes 131088
  1623.9 47.8 %reduce-scatter.44.cloned.1.call-done = bf16[2,128,3,256]{3,1,2,0:T(8,128)(2,1)} async-done(((bf16[2,1024,3,256]{3,1,2,0:T(8,128)(2,1)}), bf16[2,128,3,256]{3,1,2,0:T(8,128)(2,1)}) %reduce-scatter.44.cloned.1.call-update) | async-done | bytes 393232 | tf_op jit(solution)/shard_map/reduce_scatter | solution.py:309
  1673.7 77.2 %reduce-scatter.42.cloned.1.call-done = bf16[512,1024]{1,0:T(8,128)(2,1)} async-done(((bf16[2048,1024]{1,0:T(8,128)(2,1)}), bf16[512,1024]{1,0:T(8,128)(2,1)}) %reduce-scatter.42.cloned.1.call-update) | async-done | bytes 1048592 | tf_op jit(solution)/shard_map/reduce_scatter | solution.py:163
  1765.7 127.2 %reduce-scatter.52.cloned.1.call-done = f32[32,4]{1,0:T(8,128)} async-done(((f32[1024,4]{1,0:T(8,128)}), f32[32,4]{1,0:T(8,128)}) %reduce-scatter.52.cloned.1.call-update) | async-done | bytes 528
  1894.4 131.5 %reduce-scatter.54.cloned.1.call-done = f32[32,4]{1,0:T(8,128)} async-done(((f32[1024,4]{1,0:T(8,128)}), f32[32,4]{1,0:T(8,128)}) %reduce-scatter.54.cloned.1.call-update) | async-done | bytes 528
  (326 shorter events, 292.1 us)
Async XLA Ops:
  7.2 88.2 %all-gather.11.cloned.1.call-start = ((), (), s32[]{:S(2)}) async-start(), calls=%async_computation.21 | async-start | bytes 5242880 | tf_op jit(solution)/shard_map/all_gather | solution.py:150
  9.8 158.0 %copy-start.31 = (f32[1,1,1024]{2,1,0:T(1,128)}, f32[1,1,1024]{2,1,0:T(1,128)S(1)}, u32[]{:S(2)}) copy-start(f32[1,1,1024]{2,1,0:T(1,128)S(1)} %get-tuple-element.79) | copy-start | bytes 12292
  11.8 148.5 %all-gather.23.cloned.1.call-start = ((), (), s32[]{:S(2)}) async-start(), calls=%async_computation.37 | async-start | bytes 2621440 | tf_op jit(solution)/shard_map/all_gather | solution.py:198
  119.1 44.4 %all-to-all-start = ((bf16[4,512,256]{1,2,0:T(8,128)(2,1)}), bf16[4,512,256]{1,2,0:T(8,128)(2,1)S(1)}, u32[]{:S(2)}, u32[]{:S(2)}) async-start(bf16[4,512,256]{1,2,0:T(8,128)(2,1)} %copy.44), calls=%async_computation | async-start | bytes 2097152 | tf_op jit(solution)/shard_map/all_to_all | solution.py:199
  122.7 126.2 %all-gather.13.cloned.1.call-start = ((), (), s32[]{:S(2)}) async-start(), calls=%async_computation.22 | async-start | bytes 5242880 | tf_op jit(solution)/shard_map/all_gather | solution.py:150
  169.3 172.3 %reduce-scatter.32.cloned.1.call-start = ((), (), s32[]{:S(2)}) async-start(), calls=%async_computation.23 | async-start | bytes 5242880 | tf_op jit(solution)/shard_map/reduce_scatter | solution.py:154
  266.1 161.2 %all-gather.15.cloned.1.call-start = ((), (), s32[]{:S(2)}) async-start(), calls=%async_computation.24 | async-start | bytes 5242880 | tf_op jit(solution)/shard_map/all_gather | solution.py:150
  345.9 146.9 %all-gather.25.cloned.1.call-start = ((), (), s32[]{:S(2)}) async-start(), calls=%async_computation.38 | async-start | bytes 2621440 | tf_op jit(solution)/shard_map/all_gather | solution.py:198
  451.4 44.5 %all-to-all-start.1 = ((bf16[4,512,256]{1,2,0:T(8,128)(2,1)}), bf16[4,512,256]{1,2,0:T(8,128)(2,1)S(1)}, u32[]{:S(2)}, u32[]{:S(2)}) async-start(bf16[4,512,256]{1,2,0:T(8,128)(2,1)} %copy.46), calls=%async_computation.2 | async-start | bytes 2097152 | tf_op jit(solution)/shard_map/all_to_all | solution.py:199
  455.0 127.4 %all-gather.17.cloned.1.call-start = ((), (), s32[]{:S(2)}) async-start(), calls=%async_computation.25 | async-start | bytes 5242880 | tf_op jit(solution)/shard_map/all_gather | solution.py:150
  502.7 160.6 %all-gather.19.cloned.1.call-start = ((), (), s32[]{:S(2)}) async-start(), calls=%async_computation.27 | async-start | bytes 5242880 | tf_op jit(solution)/shard_map/all_gather | solution.py:249
  506.8 254.6 %reduce-scatter.36.cloned.1.call-start = ((), (), s32[]{:S(2)}) async-start(), calls=%async_computation.28 | async-start | bytes 5242880 | tf_op jit(solution)/shard_map/reduce_scatter | solution.py:163
  686.0 154.9 %reduce-scatter.34.cloned.1.call-start = ((), (), s32[]{:S(2)}) async-start(), calls=%async_computation.26 | async-start | bytes 5242880 | tf_op jit(solution)/shard_map/reduce_scatter | solution.py:154
  698.0 279.0 %reduce-scatter.38.cloned.1.call-start = ((), (), s32[]{:S(2)}) async-start(), calls=%async_computation.29 | async-start | bytes 5242880 | tf_op jit(solution)/shard_map/reduce_scatter | solution.py:163
  901.0 165.0 %all-gather.21.cloned.1.call-start = ((), (), s32[]{:S(2)}) async-start(), calls=%async_computation.30 | async-start | bytes 5242880 | tf_op jit(solution)/shard_map/all_gather | solution.py:249
  984.5 179.4 %reduce-scatter.40.cloned.1.call-start = ((), (), s32[]{:S(2)}) async-start(), calls=%async_computation.31 | async-start | bytes 5242880 | tf_op jit(solution)/shard_map/reduce_scatter | solution.py:163
  1088.5 209.4 %reduce-scatter.48.cloned.1.call-start = ((), (), s32[]{:S(2)}) async-start(), calls=%async_computation.35 | async-start | bytes 2621440 | tf_op jit(solution)/shard_map/reduce_scatter | solution.py:264
  1094.0 204.0 %reduce-scatter.46.cloned.1.call-start = ((), (), s32[]{:S(2)}) async-start(), calls=%async_computation.34 | async-start | bytes 2621440 | tf_op jit(solution)/shard_map/reduce_scatter | solution.py:264
  1172.2 157.3 %reduce-scatter.62.cloned.1.call-start = ((), (), s32[]{:S(2)}) async-start(), calls=%async_computation.44 | async-start | bytes 294912
  1184.0 174.3 %reduce-scatter.64.cloned.1.call-start = ((), (), s32[]{:S(2)}) async-start(), calls=%async_computation.45 | async-start | bytes 4718592
  1214.5 198.8 %reduce-scatter.50.cloned.1.call-start = ((), (), s32[]{:S(2)}) async-start(), calls=%async_computation.36 | async-start | bytes 4718592 | tf_op jit(solution)/shard_map/reduce_scatter | solution.py:318
  1236.3 40.9 %all-to-all-start.3 = ((bf16[512,4,256]{2,0,1:T(8,128)(2,1)}), bf16[512,4,256]{2,0,1:T(8,128)(2,1)S(1)}, u32[]{:S(2)}, u32[]{:S(2)}) async-start(bf16[512,4,256]{2,0,1:T(8,128)(2,1)} %bitcast.179), calls=%async_computation.8 | async-start | bytes 2097152 | tf_op jit(solution)/shard_map/all_to_all | solution.py:271
  1240.4 309.8 %reduce-scatter.56.cloned.1.call-start = ((), (), s32[]{:S(2)}) async-start(), calls=%async_computation.41 | async-start | bytes 540672
  1242.5 340.4 %reduce-scatter.58.cloned.1.call-start = ((), (), s32[]{:S(2)}) async-start(), calls=%async_computation.42 | async-start | bytes 73728
  1297.9 324.2 %reduce-scatter.60.cloned.1.call-start = ((), (), s32[]{:S(2)}) async-start(), calls=%async_computation.43 | async-start | bytes 1179648
  1301.4 370.3 %reduce-scatter.44.cloned.1.call-start = ((), (), s32[]{:S(2)}) async-start(), calls=%async_computation.33 | async-start | bytes 3538944 | tf_op jit(solution)/shard_map/reduce_scatter | solution.py:309
  1320.8 430.1 %reduce-scatter.42.cloned.1.call-start = ((), (), s32[]{:S(2)}) async-start(), calls=%async_computation.32 | async-start | bytes 5242880 | tf_op jit(solution)/shard_map/reduce_scatter | solution.py:163
  1329.2 563.7 %reduce-scatter.52.cloned.1.call-start = ((), (), s32[]{:S(2)}) async-start(), calls=%async_computation.39 | async-start | bytes 540672
  1361.3 389.5 %copy-start.3 = (f32[512,1024]{1,0:T(8,128)S(1)}, f32[512,1024]{1,0:T(8,128)}, u32[]{:S(2)}) copy-start(f32[512,1024]{1,0:T(8,128)} %param.12) | copy-start | bytes 6291460
  1361.3 389.5 %copy-start.34 = (f32[1,1,1024]{2,1,0:T(1,128)S(1)}, f32[1,1,1024]{2,1,0:T(1,128)}, u32[]{:S(2)}) copy-start(f32[1,1,1024]{2,1,0:T(1,128)} %copy-done.33) | copy-start | bytes 12292
  1361.3 389.5 %copy-start.38 = (f32[512]{0:T(512)S(1)}, f32[512]{0:T(512)}, u32[]{:S(2)}) copy-start(f32[512]{0:T(512)} %copy-done.37) | copy-start | bytes 6148
  1758.0 267.8 %reduce-scatter.54.cloned.1.call-start = ((), (), s32[]{:S(2)}) async-start(), calls=%async_computation.40 | async-start | bytes 540672
  (61 other events, 790.3 us)
Sparse Core Ops, SparseCore 0:
  11.9 83.4 all-gather.10
  97.0 63.2 all-gather.22
  169.4 79.4 all-gather.12
  266.3 75.2 reduce-scatter.31
  346.1 81.2 all-gather.14
  429.5 63.3 all-gather.24
  502.9 79.4 all-gather.16
  584.0 79.2 all-gather.18
  686.1 75.2 reduce-scatter.35
  763.6 77.2 reduce-scatter.33
  901.1 75.7 reduce-scatter.37
  984.7 81.2 all-gather.20
  1088.6 75.2 reduce-scatter.39
  1166.2 44.3 reduce-scatter.47
  1212.8 52.6 reduce-scatter.45
  1269.2 34.5 reduce-scatter.61
  1307.0 51.3 reduce-scatter.63
  1361.9 51.3 reduce-scatter.49
  1416.1 134.0 reduce-scatter.55
  1553.3 29.4 reduce-scatter.57
  1586.0 36.0 reduce-scatter.59
  1625.4 46.2 reduce-scatter.43
  1674.1 76.7 reduce-scatter.41
  1758.1 134.7 reduce-scatter.51
  1895.2 130.5 reduce-scatter.53
